TPU v7x, 256 devices: a whole 4x4x8 slice. The times are simulated.
256 devices in a mesh: chan: 8 (over y, core), bl: 32 (over x, z).
Axes of the slice: x: 4, y: 4, z: 8, core: 2. Of those that a mesh axis runs over, the one named last changes fastest.
Arguments:
- visibility: float32 [8, 64, 2, 131072], P(None, 'chan', None, 'bl')
- model_vis: float32 [8, 64, 2, 131072], P(None, 'chan', None, 'bl')
- station_pairs: int32 [2, 131072], P(None, 'bl'), may hold values from 0 to 511, as said below
- init_gains: float32 [8, 64, 512], P(None, 'chan'), may hold values from -4 to 4
Outputs:
- solved_gains: float32 [8, 64, 512], P(None, 'chan')
Inputs may be any that keep to these rules, and one draw needn't show every extreme that they name: `station_pairs`: each baseline joins two different stations; some baseline joins station 0 and station 512 - 1.
All inputs are finite; a program needn't handle non-finite values.
Results may differ from a plain program's by a relative error of at most 0.0001.
Values sent between devices are 32-bit elements; how exact they have to be, the bound alone decides.
A program may use at most 64 MiB of HBM per device.

v0:
```python
import jax
import jax.numpy as jnp
from jax import lax
from jax.sharding import PartitionSpec as P

ITERS = 3


RIDGE = 1.0


def padded_2(shard, sides, width):
    for axis, dim in sides:
        size, length = (lax.axis_size(axis), shard.shape[dim])
        up = [(i, (i + 1) % size) for i in range(size - 1)]
        down = [(j, i) for i, j in up]
        last = lax.slice_in_dim(shard, length - width, length, axis=dim)
        first = lax.slice_in_dim(shard, 0, width, axis=dim)
        before = lax.ppermute(last, axis, up)
        after = lax.ppermute(first, axis, down)
        shard = jnp.concatenate([before, shard, after], axis=dim)
    return shard


def jones_product(p, q):
    real = (
        p[0][:, 0:1] * q[0][0:1]
        + p[0][:, 1:2] * q[0][1:2]
        - p[1][:, 0:1] * q[1][0:1]
        - p[1][:, 1:2] * q[1][1:2]
    )
    imag = (
        p[0][:, 0:1] * q[1][0:1]
        + p[0][:, 1:2] * q[1][1:2]
        + p[1][:, 0:1] * q[0][0:1]
        + p[1][:, 1:2] * q[0][1:2]
    )
    return jnp.stack([real, imag])


def adjoint(p):
    return jnp.stack([jnp.swapaxes(p[0], 0, 1), -jnp.swapaxes(p[1], 0, 1)])


def lookup(jones, table):
    chan_count = jones.shape[3]
    flat = jones.reshape(8 * chan_count, jones.shape[4])
    picked = lax.dot_general(
        flat,
        table,
        (((1,), (1,)), ((), ())),
        precision=lax.Precision.HIGHEST,
        preferred_element_type=jnp.float32,
    )
    return picked.reshape(2, 2, 2, chan_count, 1, table.shape[0])


def collect(terms, table):
    rows = terms.shape[0] * terms.shape[1]
    summed = jnp.dot(
        terms.reshape(rows, terms.shape[2]),
        table,
        precision=lax.Precision.HIGHEST,
        preferred_element_type=jnp.float32,
    )
    return summed.reshape(terms.shape[0], terms.shape[1], table.shape[1])


def station_terms(vis, model, jones, table_first, table_second):
    chan_count = vis.shape[3]
    base_count = vis.shape[5]
    gain_first = lookup(jones, table_first)
    gain_second = lookup(jones, table_second)
    ahead = jones_product(model, adjoint(gain_second))
    behind = jones_product(adjoint(model), adjoint(gain_first))
    numer_first = jnp.sum(jones_product(vis, adjoint(ahead)), axis=4)
    denom_first = jnp.sum(jones_product(ahead, adjoint(ahead)), axis=4)
    numer_second = jnp.sum(jones_product(adjoint(vis), adjoint(behind)), axis=4)
    denom_second = jnp.sum(jones_product(behind, adjoint(behind)), axis=4)
    from_first = jnp.concatenate(
        [
            numer_first.reshape(8, chan_count, base_count),
            denom_first.reshape(8, chan_count, base_count),
        ]
    )
    from_second = jnp.concatenate(
        [
            numer_second.reshape(8, chan_count, base_count),
            denom_second.reshape(8, chan_count, base_count),
        ]
    )
    return collect(from_first, table_first) + collect(from_second, table_second)


def update(total, old):
    shape = old.shape
    numer = total[:8].reshape(shape)
    denom = total[8:].reshape(shape)
    upper = denom[0, 0, 0] + RIDGE
    lower = denom[0, 1, 1] + RIDGE
    off_real = denom[0, 0, 1]
    off_imag = denom[1, 0, 1]
    determinant = upper * lower - off_real * off_real - off_imag * off_imag
    zero = jnp.zeros_like(upper)
    inverse = (
        jnp.stack(
            [
                jnp.stack([jnp.stack([lower, -off_real]), jnp.stack([-off_real, upper])]),
                jnp.stack([jnp.stack([zero, -off_imag]), jnp.stack([off_imag, zero])]),
            ]
        )
        / determinant
    )
    return 0.5 * (jones_product(numer, inverse) + old)


def smooth(jones):
    shape = jones.shape
    chan_count = shape[3]
    flat = jones.reshape(8, chan_count, shape[4])
    padded = padded_2(flat, (("chan", 1),), 1)
    total = padded[:, :-2] + 2.0 * padded[:, 1:-1] + padded[:, 2:]
    index = lax.axis_index("chan") * chan_count + jnp.arange(chan_count, dtype=jnp.int32)
    last = chan_count * lax.axis_size("chan") - 1
    weight = 4.0 - (index == 0).astype(jnp.float32) - (index == last).astype(jnp.float32)
    return (total / weight[None, :, None]).reshape(shape)


def body(visibility, model_vis, station_pairs, init_gains):
    chan_count = visibility.shape[1]
    time_count = visibility.shape[2]
    base_count = visibility.shape[3]
    stat_count = init_gains.shape[2]
    vis = visibility.reshape(2, 2, 2, chan_count, time_count, base_count)
    model = model_vis.reshape(2, 2, 2, chan_count, time_count, base_count)
    stations = jnp.arange(stat_count, dtype=jnp.int32)
    table_first = (station_pairs[0][:, None] == stations[None, :]).astype(jnp.float32)
    table_second = (station_pairs[1][:, None] == stations[None, :]).astype(jnp.float32)
    jones = init_gains.reshape(2, 2, 2, chan_count, stat_count)
    for step in range(ITERS):
        sums = station_terms(vis, model, jones, table_first, table_second)
        total = lax.psum(sums, "bl")
        jones = smooth(update(total, jones))
    return jones.reshape(8, chan_count, stat_count)


def solution(mesh):
    in_specs = (
        P(None, "chan", None, "bl"),
        P(None, "chan", None, "bl"),
        P(None, "bl"),
        P(None, "chan", None),
    )
    out_specs = P(None, "chan", None)
    return jax.shard_map(body, mesh=mesh, in_specs=in_specs, out_specs=out_specs, check_vma=False)
```

profile of v0, /device:TPU:1, one launch (start us, length us, event | category | flops | bytes accessed | tf_op | source)
XLA Modules:
  0.0 569.0 jit_solution(17347076753245104788)
XLA Ops:
  7.4 5.2 fusion.20
  12.7 1.5 copy-done.30
  19.6 5.1 fusion.21
  31.1 1.1 multiply_subtract_fusion.22
  32.4 3.1 fusion.8
  37.1 17.5 %fusion.52 = f32[16,8,512]{2,1,0:T(8,128)} fusion(f32[16,8,512]{2,1,0:T(8,128)S(1)} %fusion.8, s32[4096]{0:T(1024)S(1)} %bitcast.465, f32[8,8,4096]{2,1,0:T(8,128)S(1)} %bitcast.441, f32[8,8,4096]{2,1,0:T(8,128)S(1)} %bitcast.447), kind=kOutput, calls=%fused_computation.60 | convolution fusion | flops 3223912448 | bytes 2637824 | tf_op jit(solution)/shard_map/dot_general | solution.py:60
  54.7 143.4 %all-reduce.10.cloned.1.call-done = f32[16,8,512]{2,1,0:T(8,128)} async-done(((f32[16,8,512]{2,1,0:T(8,128)}), f32[16,8,512]{2,1,0:T(8,128)}) %all-reduce.10.cloned.1.call-update) | async-done | bytes 262160 | tf_op jit(solution)/shard_map/psum | solution.py:142
  200.2 7.0 %collective-permute-start.1 = (f32[8,1,512]{2,1,0:T(1,128)S(1)}, f32[8,1,512]{2,1,0:T(1,128)S(1)}, u32[]{:S(2)}, u32[]{:S(2)}) collective-permute-start(f32[8,1,512]{2,1,0:T(1,128)S(1)} %get-tuple-element.204), channel_id=1, source_target_pairs={{32,0},{64,32},{96,64},{128,96},{160,128},{192,160},{224,192},{33,... | collective-permute-start | bytes 49160 | tf_op jit(solution)/shard_map/ppermute | solution.py:20
  207.2 3.0 collective-permute-start
  211.2 4.9 fusion.11
  217.3 4.9 fusion
  227.8 3.1 fusion.6
  230.9 1.1 multiply_subtract_fusion.10
  232.2 3.8 fusion.57
  236.0 137.2 %all-reduce.12.cloned.1.call-done = f32[16,8,512]{2,1,0:T(8,128)} async-done(((f32[16,8,512]{2,1,0:T(8,128)}), f32[16,8,512]{2,1,0:T(8,128)}) %all-reduce.12.cloned.1.call-update) | async-done | bytes 262160 | tf_op jit(solution)/shard_map/psum | solution.py:142
  375.3 7.0 %collective-permute-start.3 = (f32[8,1,512]{2,1,0:T(1,128)S(1)}, f32[8,1,512]{2,1,0:T(1,128)S(1)}, u32[]{:S(2)}, u32[]{:S(2)}) collective-permute-start(f32[8,1,512]{2,1,0:T(1,128)S(1)} %get-tuple-element.193), channel_id=1, source_target_pairs={{32,0},{64,32},{96,64},{128,96},{160,128},{192,160},{224,192},{33,... | collective-permute-start | bytes 49160 | tf_op jit(solution)/shard_map/ppermute | solution.py:20
  382.4 3.0 collective-permute-start.2
  386.3 4.9 fusion.10
  392.4 5.1 fusion.1
  403.1 3.1 fusion.4
  407.4 3.8 fusion.62
  411.2 137.2 %all-reduce.14.cloned.1.call-done = f32[16,8,512]{2,1,0:T(8,128)} async-done(((f32[16,8,512]{2,1,0:T(8,128)}), f32[16,8,512]{2,1,0:T(8,128)}) %all-reduce.14.cloned.1.call-update) | async-done | bytes 262160 | tf_op jit(solution)/shard_map/psum | solution.py:142
  550.5 7.0 %collective-permute-start.5 = (f32[8,1,512]{2,1,0:T(1,128)S(1)}, f32[8,1,512]{2,1,0:T(1,128)S(1)}, u32[]{:S(2)}, u32[]{:S(2)}) collective-permute-start(f32[8,1,512]{2,1,0:T(1,128)S(1)} %get-tuple-element.182), channel_id=1, source_target_pairs={{32,0},{64,32},{96,64},{128,96},{160,128},{192,160},{224,192},{33,... | collective-permute-start | bytes 49160 | tf_op jit(solution)/shard_map/ppermute | solution.py:20
  557.5 3.0 collective-permute-start.4
  (227 shorter events, 38.1 us)
Async XLA Ops:
  6.5 191.6 %all-reduce.10.cloned.1.call-start = ((), (), s32[]{:S(2)}) async-start(), calls=%async_computation | async-start | bytes 524288 | tf_op jit(solution)/shard_map/psum | solution.py:142
  28.0 3.0 copy-start.18
  28.3 2.7 copy-start.21
  28.8 2.3 copy-start.24
  29.5 6.3 %copy-start.6 = (f32[2,8,2,4096]{3,1,2,0:T(8,128)}, f32[2,8,2,4096]{3,1,2,0:T(8,128)S(1)}, u32[]{:S(2)}) copy-start(f32[2,8,2,4096]{3,1,2,0:T(8,128)S(1)} %copy.24) | copy-start | bytes 1572868
  29.9 6.0 %copy-start.9 = (f32[2,8,2,4096]{3,1,2,0:T(8,128)}, f32[2,8,2,4096]{3,1,2,0:T(8,128)S(1)}, u32[]{:S(2)}) copy-start(f32[2,8,2,4096]{3,1,2,0:T(8,128)S(1)} %copy.23) | copy-start | bytes 1572868
  30.3 5.5 copy-start.12
  30.6 5.2 copy-start.15
  54.7 318.6 %all-reduce.12.cloned.1.call-start = ((), (), s32[]{:S(2)}) async-start(), calls=%async_computation.1 | async-start | bytes 524288 | tf_op jit(solution)/shard_map/psum | solution.py:142
  200.2 10.1 %collective-permute-start.1 = (f32[8,1,512]{2,1,0:T(1,128)S(1)}, f32[8,1,512]{2,1,0:T(1,128)S(1)}, u32[]{:S(2)}, u32[]{:S(2)}) collective-permute-start(f32[8,1,512]{2,1,0:T(1,128)S(1)} %get-tuple-element.204), channel_id=1, source_target_pairs={{32,0},{64,32},{96,64},{128,96},{160,128},{192,160},{224,192},{33,... | collective-permute-start | bytes 49160 | tf_op jit(solution)/shard_map/ppermute | solution.py:20
  207.2 3.9 collective-permute-start
  227.7 3.1 copy-start.7
  227.7 3.1 copy-start.10
  227.7 3.1 copy-start.13
  227.8 3.1 copy-start.16
  236.0 312.4 %all-reduce.14.cloned.1.call-start = ((), (), s32[]{:S(2)}) async-start(), calls=%async_computation.2 | async-start | bytes 524288 | tf_op jit(solution)/shard_map/psum | solution.py:142
  375.3 10.0 %collective-permute-start.3 = (f32[8,1,512]{2,1,0:T(1,128)S(1)}, f32[8,1,512]{2,1,0:T(1,128)S(1)}, u32[]{:S(2)}, u32[]{:S(2)}) collective-permute-start(f32[8,1,512]{2,1,0:T(1,128)S(1)} %get-tuple-element.193), channel_id=1, source_target_pairs={{32,0},{64,32},{96,64},{128,96},{160,128},{192,160},{224,192},{33,... | collective-permute-start | bytes 49160 | tf_op jit(solution)/shard_map/ppermute | solution.py:20
  382.4 3.9 collective-permute-start.2
  403.1 3.1 copy-start.8
  403.1 3.1 copy-start.11
  403.1 3.1 copy-start.14
  403.1 3.1 copy-start.17
  550.5 10.0 %collective-permute-start.5 = (f32[8,1,512]{2,1,0:T(1,128)S(1)}, f32[8,1,512]{2,1,0:T(1,128)S(1)}, u32[]{:S(2)}, u32[]{:S(2)}) collective-permute-start(f32[8,1,512]{2,1,0:T(1,128)S(1)} %get-tuple-element.182), channel_id=1, source_target_pairs={{32,0},{64,32},{96,64},{128,96},{160,128},{192,160},{224,192},{33,... | collective-permute-start | bytes 49160 | tf_op jit(solution)/shard_map/ppermute | solution.py:20
  557.5 3.9 collective-permute-start.4
  (18 other events, 22.3 us)
Sparse Core Ops, SparseCore 0:
  54.8 143.2 all-reduce.9
  236.1 137.0 all-reduce.11
  411.3 137.0 all-reduce.13
where the time goes:
time: 576 us; the launch traced here: 569 us
  waiting for transfers between devices  420 us (73%)
  matrix products  64.4 us (11%)
  starting transfers between devices  30.1 us (5%)
  local copies, waits for them, and re-layouts  22.6 us (4%)
  other arithmetic  16.4 us (3%)
  between operations  15.1 us (3%)
    psum x3, waiting for transfers between devices, body(): total = lax.psum(sums, 'bl')  418 us
    dot_general x6, matrix products, collect(): jnp.dot(terms.reshape(rows, terms.shape[2]), table, precision=lax.Precisi...  34.2 us
    dot_general x6, matrix products, lookup(): lax.dot_general(flat, table, (((1,), (1,)), ((), ())), precision=lax.Prec...  30.2 us
    ppermute x3, starting transfers between devices, padded_2(): after = lax.ppermute(first, axis, down)  21 us
    sub x21, other arithmetic, jones_product(): p[0][:, 0:1] * q[0][0:1] + p[0][:, 1:2] * q[0][1:2]  12.4 us
  transfers between devices with their start and end apart: 9, of which 6 were waited for; matrix products, arithmetic and copies ran while one was open for 0% of the time, Pallas kernels for 0%

commit v1 on v0

v1 whole, which is shorter than its diff:
```python
import jax
import jax.numpy as jnp
from jax import lax
from jax.experimental import pallas as pl
from jax.experimental.pallas import tpu as pltpu
from jax.sharding import PartitionSpec as P

ITERS = 3
RIDGE = 1.0
NX, NZ, NCH = 4, 8, 8
NS, NB = 512, 4096
LANES = 128
MESH = pl.DeviceIdType.MESH
F32, BF16 = jnp.float32, jnp.bfloat16


def hops(off):
    return min(off[0], NX - off[0]) + min(off[1], NZ - off[1])


OFFSETS = sorted([(i, j) for i in range(NX) for j in range(NZ)], key=lambda o: -hops(o))
PEERS = [o for o in OFFSETS if o != (0, 0)]


def cmul(a, b, ca=False, cb=False):
    (ar, ai), (br, bi) = a, b
    re = ar * br + ai * bi if ca != cb else ar * br - ai * bi
    if ca:
        im = ar * bi - ai * br if not cb else -(ar * bi + ai * br)
    else:
        im = ai * br - ar * bi if cb else ar * bi + ai * br
    return re, im


def cadd(a, b):
    return a[0] + b[0], a[1] + b[1]


def mm(a, b, ah=False, bh=False):
    def one(i, j):
        parts = []
        for k in range(2):
            left = a[k][i] if ah else a[i][k]
            right = b[j][k] if bh else b[k][j]
            parts.append(cmul(left, right, ah, bh))
        return cadd(*parts)

    return [[one(i, j) for j in range(2)] for i in range(2)]


def herm(a):
    def square(z):
        return z[0] * z[0] + z[1] * z[1]

    off = cadd(cmul(a[0][0], a[1][0], cb=True), cmul(a[0][1], a[1][1], cb=True))
    return [square(a[0][0]) + square(a[0][1]), square(a[1][0]) + square(a[1][1]), off[0], off[1]]


def mat(v):
    return [[(v[2 * i + j], v[4 + 2 * i + j]) for j in range(2)] for i in range(2)]


def flat(m):
    return [m[i][j][p] for p in range(2) for i in range(2) for j in range(2)]


def station_terms(vis, model, gain_first, gain_second):
    total = None
    for t in range(2):
        v, m = mat(vis[t]), mat(model[t])
        ahead = mm(m, gain_second, bh=True)
        behind = mm(m, gain_first, ah=True, bh=True)
        new = [
            flat(mm(v, ahead, bh=True)) + herm(ahead),
            flat(mm(v, behind, ah=True, bh=True)) + herm(behind),
        ]
        total = new if total is None else [[x + y for x, y in zip(s, n)] for s, n in zip(total, new)]
    return total


def kernel(vis_hbm, model_hbm, pairs, init, out, vis, model, table_g, table_s, gains_lhs, gains, terms, acc, gs, sb, rb, gb, mine, in_sem, rs_send, rs_recv, ag_send, ag_recv):
    c, b = lax.axis_index("chan"), lax.axis_index("bl")
    x, z = b // NZ, b % NZ
    my_ch = lax.rem(z + 2 * x, NCH)

    def peer(off, dc=0):
        dx, dz = off
        return (lax.rem(c + dc + 8, 8), lax.rem(x + dx, NX) * NZ + lax.rem(z + dz, NZ))

    barrier = pltpu.get_barrier_semaphore()

    def greet(device):
        pl.semaphore_signal(barrier, inc=1, device_id=device, device_id_type=MESH)

    for i in range(NX):
        greet((lax.rem(c + 1, 8), i * NZ + lax.rem(16 - 2 * i, NZ)))
        greet((lax.rem(c + 7, 8), i * NZ + lax.rem(23 - 2 * i, NZ)))
    for off in PEERS:
        greet(peer(off))

    copies = []
    for t in range(2):
        for k in range(NCH):
            copies.append(pltpu.make_async_copy(vis_hbm.at[:, k, t, :], vis.at[t, :, k, :], in_sem.at[2 * NCH * t + k]))
            copies.append(pltpu.make_async_copy(model_hbm.at[:, k, t, :], model.at[t, :, k, :], in_sem.at[2 * NCH * t + NCH + k]))
    for copy in copies:
        copy.start()

    low = lax.broadcasted_iota(jnp.int32, (256, LANES), 0)
    wide = lax.broadcasted_iota(jnp.int32, (LANES, NS), 1).astype(F32)
    for side in range(2):

        def tables(g, _):
            lanes = pl.ds(pl.multiple_of(g * LANES, LANES), LANES)
            dst = pl.ds(pl.multiple_of(side * NB + g * LANES, LANES), LANES)
            row = pairs[side : side + 1, lanes]
            table_g[:, dst] = jnp.where(jnp.broadcast_to(row & 255, (256, LANES)) == low, 1.0, 0.0).astype(BF16)
            column = jnp.broadcast_to(row.astype(F32), (LANES, LANES)).T
            column = jnp.concatenate([column] * 4, axis=1)
            table_s[dst, :] = jnp.where(column == wide, 1.0, 0.0).astype(BF16)
            return 0

        lax.fori_loop(0, NB // LANES, tables, 0)

    for s in range(4):
        for k in range(8):
            gs[pl.ds(s * 64 + k, 8, stride=8), :] = init[k, :, s * LANES : (s + 1) * LANES]

    for copy in copies:
        copy.wait()

    def iteration(step, _):
        for s in range(4):
            rows, lanes = (s // 2) * 128, slice((s % 2) * LANES, (s % 2 + 1) * LANES)
            for k in range(0, 8, 2):
                two = jnp.concatenate([gs[pl.ds(s * 64 + k + i, 8, stride=8), :] for i in range(2)], axis=0)
                high = two.astype(BF16)
                gains_lhs[rows + 8 * k : rows + 8 * k + 16, lanes] = high
                gains_lhs[rows + 64 + 8 * k : rows + 64 + 8 * k + 16, lanes] = (two - high.astype(F32)).astype(BF16)

        width = 1024
        for side in range(2):

            def lookup(g, _):
                src = pl.ds(pl.multiple_of(g * width, width), width)
                dst = pl.ds(pl.multiple_of(side * NB + g * width, width), width)
                picked = jnp.dot(gains_lhs[...], table_g[:, dst], preferred_element_type=F32)
                upper = jnp.broadcast_to(pairs[side : side + 1, src], (128, width)) >= 256
                picked = jnp.where(upper, picked[128:], picked[:128])
                gains[:, dst] = picked[:64] + picked[64:]
                return 0

            lax.fori_loop(0, NB // width, lookup, 0)

        def compute(g, _):
            lanes = pl.ds(pl.multiple_of(g * LANES, LANES), LANES)
            later = pl.ds(pl.multiple_of(NB + g * LANES, LANES), LANES)
            v = [[vis[t, k, :, lanes] for k in range(8)] for t in range(2)]
            m = [[model[t, k, :, lanes] for k in range(8)] for t in range(2)]
            first = mat([gains[8 * k : 8 * k + 8, lanes] for k in range(8)])
            second = mat([gains[8 * k : 8 * k + 8, later] for k in range(8)])
            for dst, term in zip((lanes, later), station_terms(v, m, first, second)):
                for k in range(0, 12, 2):
                    two = jnp.concatenate([term[k], term[k + 1]], axis=0)
                    high = two.astype(BF16)
                    terms[8 * k : 8 * k + 16, dst] = high
                    terms[96 + 8 * k : 96 + 8 * k + 16, dst] = (two - high.astype(F32)).astype(BF16)
            return 0

        lax.fori_loop(0, NB // LANES, compute, 0)

        for n in range(2):
            half = slice(n * 256, n * 256 + 256)
            both = jnp.dot(terms[...], table_s[:, half], preferred_element_type=F32)
            both = both[:96] + both[96:]
            for s in range(2):
                acc[2 * n + s] = both[:, s * LANES : (s + 1) * LANES]
        for s in range(4):
            for k in range(NCH):
                sb[step, s, k] = acc[s, pl.ds(k, 12, stride=8), :]

        @pl.when(step == 0)
        def _():
            edge = jnp.where((my_ch == 0) | (my_ch == NCH - 1), 32, 0)
            pl.semaphore_wait(barrier, 31 + edge)

        for off in PEERS:
            there = peer(off)[1]
            tx, tz = there // NZ, there % NZ
            pltpu.make_async_remote_copy(
                src_ref=sb.at[step, tx, lax.rem(tz + 2 * tx, NCH)],
                dst_ref=rb.at[step, b],
                send_sem=rs_send.at[step],
                recv_sem=rs_recv.at[step],
                device_id=peer(off),
                device_id_type=MESH,
            ).start()
        rb[step, b] = sb[step, x, my_ch]
        landed = rb.at[step, pl.ds(0, 31)]
        pltpu.make_async_copy(landed, landed, rs_recv.at[step]).wait()

        total = rb[step, 0]
        for i in range(1, 32):
            total = total + rb[step, i]
        row = [total[k : k + 1, :] for k in range(12)]
        numer = mat(row[:8])
        upper, lower = row[8] + RIDGE, row[9] + RIDGE
        off_real, off_imag = row[10], row[11]
        inv = 1.0 / (upper * lower - off_real * off_real - off_imag * off_imag)
        zero = jnp.zeros_like(upper)
        inverse = [
            [(lower * inv, zero), (-off_real * inv, -off_imag * inv)],
            [(-off_real * inv, off_imag * inv), (upper * inv, zero)],
        ]
        old = gs[pl.ds(pl.multiple_of(x * 64 + my_ch * 8, 8), 8), :]
        solved = jnp.concatenate(flat(mm(numer, inverse)), axis=0)
        mine[step] = 0.5 * (solved + old)
        slot = x * 10 + my_ch + 1
        gb[step, slot] = mine[step]

        def give(device, there):
            pltpu.make_async_remote_copy(
                src_ref=mine.at[step],
                dst_ref=gb.at[step, there],
                send_sem=ag_send.at[step],
                recv_sem=ag_recv.at[step],
                device_id=device,
                device_id_type=MESH,
            ).start()

        @pl.when(my_ch == 0)
        def _():
            for off in OFFSETS:
                give(peer(off, -1), x * 10 + 9)

        @pl.when(my_ch == NCH - 1)
        def _():
            for off in OFFSETS:
                give(peer(off, 1), x * 10)

        for off in PEERS:
            give(peer(off), slot)
        landed = gb.at[step, pl.ds(0, 39)]
        pltpu.make_async_copy(landed, landed, ag_recv.at[step]).wait()

        for s in range(4):
            edge_before = jnp.where(c == 0, 0.0, gb[step, s * 10])
            edge_after = jnp.where(c == 7, 0.0, gb[step, s * 10 + 9])
            near = [edge_before] + [gb[step, s * 10 + k] for k in range(1, 9)] + [edge_after]
            for k in range(NCH):
                total = near[k] + 2.0 * near[k + 1] + near[k + 2]
                weight = 0.25
                if k == 0:
                    weight = jnp.where(c == 0, 1.0 / 3.0, 0.25)
                if k == NCH - 1:
                    weight = jnp.where(c == 7, 1.0 / 3.0, 0.25)
                gs[s * 64 + 8 * k : s * 64 + 8 * k + 8, :] = total * weight

        gone = rb.at[step, pl.ds(0, 31)]
        pltpu.make_async_copy(gone, gone, rs_send.at[step]).wait()
        gone = gb.at[step, pl.ds(0, 31)]
        pltpu.make_async_copy(gone, gone, ag_send.at[step]).wait()

        @pl.when((my_ch == 0) | (my_ch == NCH - 1))
        def _():
            gone = gb.at[step, pl.ds(0, 32)]
            pltpu.make_async_copy(gone, gone, ag_send.at[step]).wait()

        return 0

    lax.fori_loop(0, ITERS, iteration, 0)
    for s in range(4):
        for k in range(8):
            out[k, :, s * LANES : (s + 1) * LANES] = gs[pl.ds(s * 64 + k, 8, stride=8), :]


def body(visibility, model_vis, station_pairs, init_gains):
    vmem = pl.BlockSpec(memory_space=pltpu.VMEM)
    hbm = pl.BlockSpec(memory_space=pl.ANY)
    return pl.pallas_call(
        kernel,
        out_shape=jax.ShapeDtypeStruct((8, NCH, NS), F32),
        in_specs=[hbm, hbm, vmem, vmem],
        out_specs=vmem,
        scratch_shapes=[
            pltpu.VMEM((2, 8, NCH, NB), F32),
            pltpu.VMEM((2, 8, NCH, NB), F32),
            pltpu.VMEM((256, 2 * NB), BF16),
            pltpu.VMEM((2 * NB, NS), BF16),
            pltpu.VMEM((256, 256), BF16),
            pltpu.VMEM((64, 2 * NB), F32),
            pltpu.VMEM((192, 2 * NB), BF16),
            pltpu.VMEM((4, 96, LANES), F32),
            pltpu.VMEM((256, LANES), F32),
            pltpu.VMEM((ITERS, 4, NCH, 12, LANES), F32),
            pltpu.VMEM((ITERS, 32, 12, LANES), F32),
            pltpu.VMEM((ITERS, 40, 8, LANES), F32),
            pltpu.VMEM((ITERS, 8, LANES), F32),
            pltpu.SemaphoreType.DMA((32,)),
            pltpu.SemaphoreType.DMA((ITERS,)),
            pltpu.SemaphoreType.DMA((ITERS,)),
            pltpu.SemaphoreType.DMA((ITERS,)),
            pltpu.SemaphoreType.DMA((ITERS,)),
        ],
        compiler_params=pltpu.CompilerParams(collective_id=0, has_side_effects=True, vmem_limit_bytes=56 << 20),
    )(visibility, model_vis, station_pairs, init_gains)


def solution(mesh):
    in_specs = (
        P(None, "chan", None, "bl"),
        P(None, "chan", None, "bl"),
        P(None, "bl"),
        P(None, "chan", None),
    )
    return jax.shard_map(body, mesh=mesh, in_specs=in_specs, out_specs=P(None, "chan", None), check_vma=False)
```

time: 576 us -> 84.7 us (0.15); the launches traced: 569 us -> 84.6 us
  waiting for transfers between devices: 420 us -> 0 us
  Pallas kernels: 0 us -> 83 us
  matrix products: 64.4 us -> 0 us
  starting transfers between devices: 30.1 us -> 0 us
  local copies, waits for them, and re-layouts: 22.6 us -> 1.57 us
  other arithmetic: 16.4 us -> 0 us
  between operations: 15.1 us -> 0.01 us
    psum x3 -> x0, waiting for transfers between devices: 418 us -> none  [body(): total = lax.psum(sums, 'bl')]
    pallas_call x0 -> x1, Pallas kernels: none -> 83 us  [body(): pl.pallas_call(kernel, out_shape=jax.ShapeDtypeStruct((8, NCH, NS), F32),...]
    dot_general x12 -> x0, matrix products: 64.4 us -> none  [the longest x6 34.2 us: collect(): jnp.dot(terms.reshape(rows, terms.shape[2]), table, precision=lax.Precisi...]
    ppermute x6 -> x0, starting transfers between devices: 30.1 us -> none  [the longest x3 21 us: padded_2(): after = lax.ppermute(first, axis, down)]
    sub x22 -> x0, other arithmetic: 12.4 us -> none  [the longest x21 12.4 us: jones_product(): p[0][:, 0:1] * q[0][0:1] + p[0][:, 1:2] * q[0][1:2]]
    mul x65 -> x0, local copies, waits for them, and re-layouts: 8.06 us -> none  [the longest x29 3.13 us: jones_product(): p[1][:, 0:1] * q[1][0:1]]
    slice x12 -> x0, local copies, waits for them, and re-layouts: 6.68 us -> none  [the longest x5 3.01 us: jones_product(): p[0][:, 0:1] * q[0][0:1] + p[0][:, 1:2] * q[0][1:2]]
    unnamed x66 -> x1, local copies, waits for them, and re-layouts: 7.8 us -> 1.57 us
  transfers between devices with their start and end apart: 9 -> 0, of which waited for: 6 -> 0; matrix products, arithmetic and copies ran while one was open for 0% -> 0% of each run, Pallas kernels for 0% -> 0%
where the time goes in v1:
time: 84.7 us; the launch traced here: 84.6 us
  Pallas kernels  83 us (98%)
  local copies, waits for them, and re-layouts  1.57 us (2%)
    pallas_call x1, Pallas kernels, body(): pl.pallas_call(kernel, out_shape=jax.ShapeDtypeStruct((8, NCH, NS), F32),...  83 us

profile of v1, /device:TPU:1, one launch (start us, length us, event | category | flops | bytes accessed | tf_op | source)
XLA Modules:
  0.0 84.6 jit_solution(11713486306337503593)
XLA Ops:
  0.0 83.0 %shard_map.46 = f32[8,8,512]{2,1,0:T(8,128)} custom-call(f32[8,8,2,4096]{3,2,1,0:T(2,128)} %vis_hbm.1, f32[8,8,2,4096]{3,2,1,0:T(2,128)} %model_hbm.1, s32[2,4096]{1,0:T(2,128)} %pairs.1, f32[8,8,512]{2,1,0:T(8,128)} %init.1), custom_call_target="tpu_custom_call" | custom-call | tf_op jit(solution)/shard_map/pallas_call | solution.py:280
  83.0 1.6 %copy.6 = f32[8,8,512]{2,1,0:T(8,128)} copy(f32[8,8,512]{2,1,0:T(8,128)} %shard_map.46) | data formatting | bytes 262144

commit v2 on v1

--- a/solution.py
+++ b/solution.py
@@ -1,3 +1,5 @@
+import functools
+
 import jax
 import jax.numpy as jnp
 from jax import lax
@@ -10,6 +12,8 @@
 NX, NZ, NCH = 4, 8, 8
 NS, NB = 512, 4096
 LANES = 128
+W = 1024
+CHUNKS = NB // W
 MESH = pl.DeviceIdType.MESH
 F32, BF16 = jnp.float32, jnp.bfloat16
 
@@ -48,12 +52,14 @@
     return [[one(i, j) for j in range(2)] for i in range(2)]
 
 
-def herm(a):
-    def square(z):
-        return z[0] * z[0] + z[1] * z[1]
-
-    off = cadd(cmul(a[0][0], a[1][0], cb=True), cmul(a[0][1], a[1][1], cb=True))
-    return [square(a[0][0]) + square(a[0][1]), square(a[1][0]) + square(a[1][1]), off[0], off[1]]
+def square(z):
+    return z[0] * z[0] + z[1] * z[1]
+
+
+def tree(terms):
+    while len(terms) > 1:
+        terms = [terms[i] + terms[i + 1] for i in range(0, len(terms), 2)]
+    return terms[0]
 
 
 def mat(v):
@@ -64,24 +70,72 @@
     return [m[i][j][p] for p in range(2) for i in range(2) for j in range(2)]
 
 
-def station_terms(vis, model, gain_first, gain_second):
-    total = None
-    for t in range(2):
-        v, m = mat(vis[t]), mat(model[t])
-        ahead = mm(m, gain_second, bh=True)
-        behind = mm(m, gain_first, ah=True, bh=True)
-        new = [
-            flat(mm(v, ahead, bh=True)) + herm(ahead),
-            flat(mm(v, behind, ah=True, bh=True)) + herm(behind),
-        ]
-        total = new if total is None else [[x + y for x, y in zip(s, n)] for s, n in zip(total, new)]
-    return total
-
-
-def kernel(vis_hbm, model_hbm, pairs, init, out, vis, model, table_g, table_s, gains_lhs, gains, terms, acc, gs, sb, rb, gb, mine, in_sem, rs_send, rs_recv, ag_send, ag_recv):
+def over_time(one):
+    return cadd(one(0), one(1))
+
+
+def products(vis, model):
+    v, m = [mat(a) for a in vis], [mat(a) for a in model]
+    numer = [
+        over_time(lambda t: cmul(v[t][i][j], m[t][l][k], cb=True))
+        for i in range(2) for j in range(2) for l in range(2) for k in range(2)
+    ]
+
+    def cross(a, b):
+        return over_time(lambda t: cmul(m[t][a[0]][a[1]], m[t][b[0]][b[1]], cb=True))
+
+    power = [square(m[0][i][j]) + square(m[1][i][j]) for i in range(2) for j in range(2)]
+    u, w = cross((0, 0), (1, 1)), cross((0, 1), (1, 0))
+    pairs = [cross((0, 0), (0, 1)), cross((1, 0), (1, 1)), cross((0, 0), (1, 0)), cross((0, 1), (1, 1))]
+    mixed = [u[0] + w[0], w[1] - u[1], u[1] + w[1], u[0] - w[0]]
+    return numer, power + [part for pair in pairs for part in pair] + mixed
+
+
+def side_terms(side, numer, denom, gain):
+    rows = []
+    for i in range(2):
+        for l in range(2):
+            re, im = [], []
+            for j in range(2):
+                for k in range(2):
+                    cr, ci = numer(i, j, l, k) if side == 0 else numer(j, i, k, l)
+                    gr, gi = gain[j][k]
+                    if side == 0:
+                        re.append(cr * gr - ci * gi)
+                        im.append(cr * gi + ci * gr)
+                    else:
+                        re.append(cr * gr + ci * gi)
+                        im.append(cr * gi - ci * gr)
+            rows.append((tree(re), tree(im)))
+    out = [r[0] for r in rows] + [r[1] for r in rows]
+    h00, h11 = square(gain[0][0]) + square(gain[1][0]), square(gain[0][1]) + square(gain[1][1])
+    hr, hi = cadd(cmul(gain[0][0], gain[0][1], ca=True), cmul(gain[1][0], gain[1][1], ca=True))
+    h2r, h2i = hr + hr, hi + hi
+    d = [denom(n) for n in range(16)]
+    if side == 0:
+        out.append((d[0] * h00 + d[1] * h11) + (d[4] * h2r - d[5] * h2i))
+        out.append((d[2] * h00 + d[3] * h11) + (d[6] * h2r - d[7] * h2i))
+        out.append((d[8] * h00 + d[10] * h11) + (d[12] * hr + d[13] * hi))
+        out.append((d[9] * h00 + d[11] * h11) + (d[14] * hr + d[15] * hi))
+    else:
+        out.append((d[0] * h00 + d[2] * h11) + (d[8] * h2r + d[9] * h2i))
+        out.append((d[1] * h00 + d[3] * h11) + (d[10] * h2r + d[11] * h2i))
+        out.append((d[4] * h00 + d[6] * h11) + (d[12] * hr + d[14] * hi))
+        out.append((d[13] * hr + d[15] * hi) - (d[5] * h00 + d[7] * h11))
+    return out
+
+
+def kernel(vis_hbm, model_hbm, pairs, init, out, vis, model, numer, denom, table, table_t, gains_lhs, gains0, gains1, terms0, terms1, acc, acc4, gs, sb, rb, gb, mine, in_sem, rs_send, rs_recv, ag_send, ag_recv):
     c, b = lax.axis_index("chan"), lax.axis_index("bl")
     x, z = b // NZ, b % NZ
-    my_ch = lax.rem(z + 2 * x, NCH)
+    def owned(x, z, c):
+        place = lax.rem(z + x + 2 * (c % 2), NCH)
+        return jnp.where(place < 4, place, jnp.where(place == 4, NCH - 1, place - 1))
+
+    def edge_owner(x, c, last):
+        return lax.rem(16 + 4 * last - x - 2 * (c % 2), NZ)
+
+    my_ch = owned(x, z, c)
 
     def peer(off, dc=0):
         dx, dz = off
@@ -93,8 +147,8 @@
         pl.semaphore_signal(barrier, inc=1, device_id=device, device_id_type=MESH)
 
     for i in range(NX):
-        greet((lax.rem(c + 1, 8), i * NZ + lax.rem(16 - 2 * i, NZ)))
-        greet((lax.rem(c + 7, 8), i * NZ + lax.rem(23 - 2 * i, NZ)))
+        greet((lax.rem(c + 1, 8), i * NZ + edge_owner(i, c + 1, 0)))
+        greet((lax.rem(c + 7, 8), i * NZ + edge_owner(i, c + 1, 1)))
     for off in PEERS:
         greet(peer(off))
 
@@ -106,21 +160,28 @@
     for copy in copies:
         copy.start()
 
-    low = lax.broadcasted_iota(jnp.int32, (256, LANES), 0)
-    wide = lax.broadcasted_iota(jnp.int32, (LANES, NS), 1).astype(F32)
-    for side in range(2):
-
-        def tables(g, _):
-            lanes = pl.ds(pl.multiple_of(g * LANES, LANES), LANES)
-            dst = pl.ds(pl.multiple_of(side * NB + g * LANES, LANES), LANES)
-            row = pairs[side : side + 1, lanes]
-            table_g[:, dst] = jnp.where(jnp.broadcast_to(row & 255, (256, LANES)) == low, 1.0, 0.0).astype(BF16)
-            column = jnp.broadcast_to(row.astype(F32), (LANES, LANES)).T
-            column = jnp.concatenate([column] * 4, axis=1)
-            table_s[dst, :] = jnp.where(column == wide, 1.0, 0.0).astype(BF16)
-            return 0
-
-        lax.fori_loop(0, NB // LANES, tables, 0)
+    low = lax.broadcasted_iota(jnp.int32, (256, LANES), 0).astype(F32).astype(BF16)
+    one, nil = jnp.ones((256, LANES), BF16), jnp.zeros((256, LANES), BF16)
+    across = lax.broadcasted_iota(jnp.int32, (LANES, 256), 1).astype(F32).astype(BF16)
+    one_t, nil_t = jnp.ones((LANES, 256), BF16), jnp.zeros((LANES, 256), BF16)
+
+    def tables(g, _):
+        src = pl.ds(pl.multiple_of(g * LANES, LANES), LANES)
+        for side in range(2):
+            per = W // LANES
+            dst = pl.ds(pl.multiple_of((2 * (g // per) + side) * W + g % per * LANES, LANES), LANES)
+            station = pairs[side : side + 1, src]
+            row = (station & 255).astype(F32)
+            rows = jnp.concatenate([jnp.broadcast_to(row, (16, LANES)).astype(BF16)] * 16, axis=0)
+            table[:, dst] = jnp.where(rows == low, one, nil)
+            for half in range(2):
+                inside = station >= 256 if half else station < 256
+                column = jnp.broadcast_to(jnp.where(inside, row, -1.0), (LANES, LANES)).T.astype(BF16)
+                column = jnp.concatenate([column] * 2, axis=1)
+                table_t[dst, half * 256 : half * 256 + 256] = jnp.where(column == across, one_t, nil_t)
+        return 0
+
+    lax.fori_loop(0, NB // LANES, tables, 0)
 
     for s in range(4):
         for k in range(8):
@@ -128,6 +189,19 @@
 
     for copy in copies:
         copy.wait()
+
+    def prepare(g, _):
+        lanes = pl.ds(pl.multiple_of(g * LANES, LANES), LANES)
+        v = [[vis[t, k, :, lanes] for k in range(8)] for t in range(2)]
+        m = [[model[t, k, :, lanes] for k in range(8)] for t in range(2)]
+        for_numer, for_denom = products(v, m)
+        for n in range(16):
+            numer[0, n, :, lanes] = for_numer[n][0]
+            numer[1, n, :, lanes] = for_numer[n][1]
+            denom[n, :, lanes] = for_denom[n]
+        return 0
+
+    lax.fori_loop(0, NB // LANES, prepare, 0)
 
     def iteration(step, _):
         for s in range(4):
@@ -138,46 +212,63 @@
                 gains_lhs[rows + 8 * k : rows + 8 * k + 16, lanes] = high
                 gains_lhs[rows + 64 + 8 * k : rows + 64 + 8 * k + 16, lanes] = (two - high.astype(F32)).astype(BF16)
 
-        width = 1024
+        def lookup(i, side, gains):
+            picked = jnp.dot(gains_lhs[...], table[:, (2 * i + side) * W : (2 * i + side + 1) * W], preferred_element_type=F32)
+            for g in range(W // LANES):
+                lanes = slice(i * W + g * LANES, i * W + (g + 1) * LANES)
+                at = slice(g * LANES, (g + 1) * LANES)
+                upper = jnp.broadcast_to(pairs[side : side + 1, lanes], (128, LANES)) >= 256
+                chosen = jnp.where(upper, picked[128:, at], picked[:128, at])
+                gains[:, side * W + g * LANES : side * W + (g + 1) * LANES] = chosen[:64] + chosen[64:]
+
+        def compute(i, side, g, gains, terms):
+            lanes = slice(i * W + g * LANES, i * W + (g + 1) * LANES)
+            here = slice(side * W + g * LANES, side * W + (g + 1) * LANES)
+            other = slice((1 - side) * W + g * LANES, (1 - side) * W + (g + 1) * LANES)
+            gain = mat([gains[8 * k : 8 * k + 8, other] for k in range(8)])
+
+            def pick(i, j, l, k):
+                n = 8 * i + 4 * j + 2 * l + k
+                return numer[0, n, :, lanes], numer[1, n, :, lanes]
+
+            term = side_terms(side, pick, lambda n: denom[n, :, lanes], gain)
+            for k in range(0, 12, 2):
+                two = jnp.concatenate([term[k], term[k + 1]], axis=0)
+                high = two.astype(BF16)
+                terms[8 * k : 8 * k + 16, here] = high
+                terms[96 + 8 * k : 112 + 8 * k, here] = (two - high.astype(F32)).astype(BF16)
+
+        def collect(i, half, terms):
+            columns = slice(half * 256, half * 256 + 256)
+            found = jnp.dot(terms[...], table_t[2 * i * W : 2 * (i + 1) * W, columns], preferred_element_type=F32)
+            if i == 0:
+                acc[:, columns] = found
+            else:
+                acc[:, columns] += found
+
+        gains, terms = (gains0, gains1), (terms0, terms1)
         for side in range(2):
-
-            def lookup(g, _):
-                src = pl.ds(pl.multiple_of(g * width, width), width)
-                dst = pl.ds(pl.multiple_of(side * NB + g * width, width), width)
-                picked = jnp.dot(gains_lhs[...], table_g[:, dst], preferred_element_type=F32)
-                upper = jnp.broadcast_to(pairs[side : side + 1, src], (128, width)) >= 256
-                picked = jnp.where(upper, picked[128:], picked[:128])
-                gains[:, dst] = picked[:64] + picked[64:]
-                return 0
-
-            lax.fori_loop(0, NB // width, lookup, 0)
-
-        def compute(g, _):
-            lanes = pl.ds(pl.multiple_of(g * LANES, LANES), LANES)
-            later = pl.ds(pl.multiple_of(NB + g * LANES, LANES), LANES)
-            v = [[vis[t, k, :, lanes] for k in range(8)] for t in range(2)]
-            m = [[model[t, k, :, lanes] for k in range(8)] for t in range(2)]
-            first = mat([gains[8 * k : 8 * k + 8, lanes] for k in range(8)])
-            second = mat([gains[8 * k : 8 * k + 8, later] for k in range(8)])
-            for dst, term in zip((lanes, later), station_terms(v, m, first, second)):
-                for k in range(0, 12, 2):
-                    two = jnp.concatenate([term[k], term[k + 1]], axis=0)
-                    high = two.astype(BF16)
-                    terms[8 * k : 8 * k + 16, dst] = high
-                    terms[96 + 8 * k : 96 + 8 * k + 16, dst] = (two - high.astype(F32)).astype(BF16)
-            return 0
-
-        lax.fori_loop(0, NB // LANES, compute, 0)
-
-        for n in range(2):
-            half = slice(n * 256, n * 256 + 256)
-            both = jnp.dot(terms[...], table_s[:, half], preferred_element_type=F32)
-            both = both[:96] + both[96:]
-            for s in range(2):
-                acc[2 * n + s] = both[:, s * LANES : (s + 1) * LANES]
+            lookup(0, side, gains0)
+        for i in range(CHUNKS):
+            matrix = []
+            if i + 1 < CHUNKS:
+                matrix += [functools.partial(lookup, i + 1, side, gains[(i + 1) % 2]) for side in range(2)]
+            if i > 0:
+                matrix += [functools.partial(collect, i - 1, half, terms[(i + 1) % 2]) for half in range(2)]
+            vector = [(side, g) for g in range(W // LANES) for side in range(2)]
+            share = len(vector) // len(matrix)
+            for n, part in enumerate(matrix):
+                part()
+                for side, g in vector[n * share : (n + 1) * share]:
+                    compute(i, side, g, gains[i % 2], terms[i % 2])
+        for half in range(2):
+            collect(CHUNKS - 1, half, terms[(CHUNKS - 1) % 2])
+        for s in range(4):
+            lanes = slice(s * LANES, (s + 1) * LANES)
+            acc4[s] = acc[:96, lanes] + acc[96:, lanes]
         for s in range(4):
             for k in range(NCH):
-                sb[step, s, k] = acc[s, pl.ds(k, 12, stride=8), :]
+                sb[step, s, k] = acc4[s, pl.ds(k, 12, stride=8), :]
 
         @pl.when(step == 0)
         def _():
@@ -188,7 +279,7 @@
             there = peer(off)[1]
             tx, tz = there // NZ, there % NZ
             pltpu.make_async_remote_copy(
-                src_ref=sb.at[step, tx, lax.rem(tz + 2 * tx, NCH)],
+                src_ref=sb.at[step, tx, owned(tx, tz, c)],
                 dst_ref=rb.at[step, b],
                 send_sem=rs_send.at[step],
                 recv_sem=rs_recv.at[step],
@@ -203,7 +294,7 @@
         for i in range(1, 32):
             total = total + rb[step, i]
         row = [total[k : k + 1, :] for k in range(12)]
-        numer = mat(row[:8])
+        num = mat(row[:8])
         upper, lower = row[8] + RIDGE, row[9] + RIDGE
         off_real, off_imag = row[10], row[11]
         inv = 1.0 / (upper * lower - off_real * off_real - off_imag * off_imag)
@@ -213,7 +304,7 @@
             [(-off_real * inv, off_imag * inv), (upper * inv, zero)],
         ]
         old = gs[pl.ds(pl.multiple_of(x * 64 + my_ch * 8, 8), 8), :]
-        solved = jnp.concatenate(flat(mm(numer, inverse)), axis=0)
+        solved = jnp.concatenate(flat(mm(num, inverse)), axis=0)
         mine[step] = 0.5 * (solved + old)
         slot = x * 10 + my_ch + 1
         gb[step, slot] = mine[step]
@@ -228,18 +319,22 @@
                 device_id_type=MESH,
             ).start()
 
-        @pl.when(my_ch == 0)
+        for ch, dc, there in ((0, -1, x * 10 + 9), (NCH - 1, 1, x * 10)):
+
+            @pl.when(my_ch == ch)
+            def _():
+                for far in range(7, -1, -1):
+                    for off in OFFSETS:
+                        if hops(off) + 1 == far:
+                            give(peer(off, dc), there)
+                        if hops(off) == far and far > 0:
+                            give(peer(off), slot)
+
+        @pl.when((my_ch > 0) & (my_ch < NCH - 1))
         def _():
-            for off in OFFSETS:
-                give(peer(off, -1), x * 10 + 9)
-
-        @pl.when(my_ch == NCH - 1)
-        def _():
-            for off in OFFSETS:
-                give(peer(off, 1), x * 10)
-
-        for off in PEERS:
-            give(peer(off), slot)
+            for off in PEERS:
+                give(peer(off), slot)
+
         landed = gb.at[step, pl.ds(0, 39)]
         pltpu.make_async_copy(landed, landed, ag_recv.at[step]).wait()
 
@@ -285,11 +380,16 @@
         scratch_shapes=[
             pltpu.VMEM((2, 8, NCH, NB), F32),
             pltpu.VMEM((2, 8, NCH, NB), F32),
+            pltpu.VMEM((2, 16, NCH, NB), F32),
+            pltpu.VMEM((16, NCH, NB), F32),
             pltpu.VMEM((256, 2 * NB), BF16),
             pltpu.VMEM((2 * NB, NS), BF16),
             pltpu.VMEM((256, 256), BF16),
-            pltpu.VMEM((64, 2 * NB), F32),
-            pltpu.VMEM((192, 2 * NB), BF16),
+            pltpu.VMEM((64, 2 * W), F32),
+            pltpu.VMEM((64, 2 * W), F32),
+            pltpu.VMEM((192, 2 * W), BF16),
+            pltpu.VMEM((192, 2 * W), BF16),
+            pltpu.VMEM((192, NS), F32),
             pltpu.VMEM((4, 96, LANES), F32),
             pltpu.VMEM((256, LANES), F32),
             pltpu.VMEM((ITERS, 4, NCH, 12, LANES), F32),

time: 84.7 us -> 73.9 us (0.87)
  Pallas kernels: 83 us -> 72.2 us
    pallas_call x1, Pallas kernels: 83 us -> 72.2 us  [body(): pl.pallas_call(kernel, out_shape=jax.ShapeDtypeStruct((8, NCH, NS), F32),...]
where the time goes in v2:
time: 73.9 us; the launch traced here: 73.8 us
  Pallas kernels  72.2 us (98%)
  local copies, waits for them, and re-layouts  1.57 us (2%)
    pallas_call x1, Pallas kernels, body(): pl.pallas_call(kernel, out_shape=jax.ShapeDtypeStruct((8, NCH, NS), F32),...  72.2 us
    unnamed x1, local copies, waits for them, and re-layouts  1.57 us

profile of v2, /device:TPU:1, one launch (start us, length us, event | category | flops | bytes accessed | tf_op | source)
XLA Modules:
  0.0 73.8 jit_solution(14690413924380112514)
XLA Ops:
  0.0 72.2 %shard_map.46 = f32[8,8,512]{2,1,0:T(8,128)} custom-call(f32[8,8,2,4096]{3,2,1,0:T(2,128)} %vis_hbm.1, f32[8,8,2,4096]{3,2,1,0:T(2,128)} %model_hbm.1, s32[2,4096]{1,0:T(2,128)} %pairs.1, f32[8,8,512]{2,1,0:T(8,128)} %init.1), custom_call_target="tpu_custom_call" | custom-call | tf_op jit(solution)/shard_map/pallas_call | solution.py:375
  72.2 1.6 %copy.6 = f32[8,8,512]{2,1,0:T(8,128)} copy(f32[8,8,512]{2,1,0:T(8,128)} %shard_map.46) | data formatting | bytes 262144

commit v3 on v2

--- a/solution.py
+++ b/solution.py
@@ -125,7 +125,7 @@
     return out
 
 
-def kernel(vis_hbm, model_hbm, pairs, init, out, vis, model, numer, denom, table, table_t, gains_lhs, gains0, gains1, terms0, terms1, acc, acc4, gs, sb, rb, gb, mine, in_sem, rs_send, rs_recv, ag_send, ag_recv):
+def kernel(vis_hbm, model_hbm, pairs, init, out, vis, model, numer, denom, table, table_t, gains_lhs, gains0, gains1, terms0, terms1, terms2, terms3, acc, acc4, gs, sb, rb, gb, mine, in_sem, rs_send, rs_recv, ag_send, ag_recv):
     c, b = lax.axis_index("chan"), lax.axis_index("bl")
     x, z = b // NZ, b % NZ
     def owned(x, z, c):
@@ -174,11 +174,11 @@
             row = (station & 255).astype(F32)
             rows = jnp.concatenate([jnp.broadcast_to(row, (16, LANES)).astype(BF16)] * 16, axis=0)
             table[:, dst] = jnp.where(rows == low, one, nil)
+            column = jnp.broadcast_to(station.astype(F32), (LANES, LANES)).T
             for half in range(2):
-                inside = station >= 256 if half else station < 256
-                column = jnp.broadcast_to(jnp.where(inside, row, -1.0), (LANES, LANES)).T.astype(BF16)
-                column = jnp.concatenate([column] * 2, axis=1)
-                table_t[dst, half * 256 : half * 256 + 256] = jnp.where(column == across, one_t, nil_t)
+                inside = (column - 256.0 * half).astype(BF16)
+                inside = jnp.concatenate([inside] * 2, axis=1)
+                table_t[dst, half * 256 : half * 256 + 256] = jnp.where(inside == across, one_t, nil_t)
         return 0
 
     lax.fori_loop(0, NB // LANES, tables, 0)
@@ -238,15 +238,25 @@
                 terms[8 * k : 8 * k + 16, here] = high
                 terms[96 + 8 * k : 112 + 8 * k, here] = (two - high.astype(F32)).astype(BF16)
 
-        def collect(i, half, terms):
-            columns = slice(half * 256, half * 256 + 256)
-            found = jnp.dot(terms[...], table_t[2 * i * W : 2 * (i + 1) * W, columns], preferred_element_type=F32)
+        def collect(i, half):
+            columns = pl.ds(pl.multiple_of(half * 256, 256), 256)
+            return jnp.dot(terms[i][...], table_t[2 * i * W : 2 * (i + 1) * W, columns], preferred_element_type=F32)
+
+        def collect_far(i):
             if i == 0:
-                acc[:, columns] = found
+                acc[...] = collect(i, far_half)
             else:
-                acc[:, columns] += found
-
-        gains, terms = (gains0, gains1), (terms0, terms1)
+                acc[...] += collect(i, far_half)
+
+        def stage(sums, half, at):
+            for s in range(2):
+                lanes = slice(s * LANES, (s + 1) * LANES)
+                acc4[at + s] = sums[:96, lanes] + sums[96:, lanes]
+                for k in range(NCH):
+                    sb[step, 2 * half + s, k] = acc4[at + s, pl.ds(k, 12, stride=8), :]
+
+        far_half = 1 - x // 2
+        gains, terms = (gains0, gains1), (terms0, terms1, terms2, terms3)
         for side in range(2):
             lookup(0, side, gains0)
         for i in range(CHUNKS):
@@ -254,38 +264,47 @@
             if i + 1 < CHUNKS:
                 matrix += [functools.partial(lookup, i + 1, side, gains[(i + 1) % 2]) for side in range(2)]
             if i > 0:
-                matrix += [functools.partial(collect, i - 1, half, terms[(i + 1) % 2]) for half in range(2)]
+                matrix.append(functools.partial(collect_far, i - 1))
             vector = [(side, g) for g in range(W // LANES) for side in range(2)]
-            share = len(vector) // len(matrix)
+            share = -(-len(vector) // len(matrix))
             for n, part in enumerate(matrix):
                 part()
                 for side, g in vector[n * share : (n + 1) * share]:
-                    compute(i, side, g, gains[i % 2], terms[i % 2])
-        for half in range(2):
-            collect(CHUNKS - 1, half, terms[(CHUNKS - 1) % 2])
-        for s in range(4):
-            lanes = slice(s * LANES, (s + 1) * LANES)
-            acc4[s] = acc[:96, lanes] + acc[96:, lanes]
-        for s in range(4):
-            for k in range(NCH):
-                sb[step, s, k] = acc4[s, pl.ds(k, 12, stride=8), :]
+                    compute(i, side, g, gains[i % 2], terms[i])
+        stage(acc[...] + collect(CHUNKS - 1, far_half), far_half, 0)
 
         @pl.when(step == 0)
         def _():
             edge = jnp.where((my_ch == 0) | (my_ch == NCH - 1), 32, 0)
             pl.semaphore_wait(barrier, 31 + edge)
 
-        for off in PEERS:
-            there = peer(off)[1]
-            tx, tz = there // NZ, there % NZ
+        def send_sums(dx, dz):
+            device = peer((dx, dz))
+            tx, tz = device[1] // NZ, device[1] % NZ
             pltpu.make_async_remote_copy(
                 src_ref=sb.at[step, tx, owned(tx, tz, c)],
                 dst_ref=rb.at[step, b],
                 send_sem=rs_send.at[step],
                 recv_sem=rs_recv.at[step],
-                device_id=peer(off),
+                device_id=device,
                 device_id_type=MESH,
             ).start()
+
+        to_far, to_near = 3 - 2 * (x % 2), 1 + 2 * (x % 2)
+        for count in range(6, 0, -1):
+            for dz in range(NZ):
+                if hops((2, dz)) == count:
+                    send_sums(2, dz)
+                if hops((1, dz)) == count:
+                    send_sums(to_far, dz)
+        near_half = 1 - far_half
+        stage(functools.reduce(jnp.add, [collect(i, near_half) for i in range(CHUNKS)]), near_half, 2)
+        for count in range(5, 0, -1):
+            for dz in range(NZ):
+                if hops((1, dz)) == count:
+                    send_sums(to_near, dz)
+                if hops((0, dz)) == count:
+                    send_sums(0, dz)
         rb[step, b] = sb[step, x, my_ch]
         landed = rb.at[step, pl.ds(0, 31)]
         pltpu.make_async_copy(landed, landed, rs_recv.at[step]).wait()
@@ -389,7 +408,9 @@
             pltpu.VMEM((64, 2 * W), F32),
             pltpu.VMEM((192, 2 * W), BF16),
             pltpu.VMEM((192, 2 * W), BF16),
-            pltpu.VMEM((192, NS), F32),
+            pltpu.VMEM((192, 2 * W), BF16),
+            pltpu.VMEM((192, 2 * W), BF16),
+            pltpu.VMEM((192, 256), F32),
             pltpu.VMEM((4, 96, LANES), F32),
             pltpu.VMEM((256, LANES), F32),
             pltpu.VMEM((ITERS, 4, NCH, 12, LANES), F32),

time: 73.9 us -> 71.1 us (0.962)
  Pallas kernels: 72.2 us -> 69.4 us
    pallas_call x1, Pallas kernels: 72.2 us -> 69.4 us  [body(): pl.pallas_call(kernel, out_shape=jax.ShapeDtypeStruct((8, NCH, NS), F32),...]
where the time goes in v3:
time: 71.1 us; the launch traced here: 70.9 us
  Pallas kernels  69.4 us (98%)
  local copies, waits for them, and re-layouts  1.57 us (2%)
    pallas_call x1, Pallas kernels, body(): pl.pallas_call(kernel, out_shape=jax.ShapeDtypeStruct((8, NCH, NS), F32),...  69.4 us
    unnamed x1, local copies, waits for them, and re-layouts  1.57 us

profile of v3, /device:TPU:1, one launch (start us, length us, event | category | flops | bytes accessed | tf_op | source)
XLA Modules:
  0.0 70.9 jit_solution(14856233736678317275)
XLA Ops:
  0.0 69.4 %shard_map.46 = f32[8,8,512]{2,1,0:T(8,128)} custom-call(f32[8,8,2,4096]{3,2,1,0:T(2,128)} %vis_hbm.1, f32[8,8,2,4096]{3,2,1,0:T(2,128)} %model_hbm.1, s32[2,4096]{1,0:T(2,128)} %pairs.1, f32[8,8,512]{2,1,0:T(8,128)} %init.1), custom_call_target="tpu_custom_call" | custom-call | tf_op jit(solution)/shard_map/pallas_call | solution.py:394
  69.4 1.6 %copy.6 = f32[8,8,512]{2,1,0:T(8,128)} copy(f32[8,8,512]{2,1,0:T(8,128)} %shard_map.46) | data formatting | bytes 262144

commit v4 on v3

--- a/solution.py
+++ b/solution.py
@@ -181,7 +181,7 @@
                 table_t[dst, half * 256 : half * 256 + 256] = jnp.where(inside == across, one_t, nil_t)
         return 0
 
-    lax.fori_loop(0, NB // LANES, tables, 0)
+    lax.fori_loop(0, NB // LANES, tables, 0, unroll=2)
 
     for s in range(4):
         for k in range(8):

time: 71.1 us -> 69.9 us (0.983)
  Pallas kernels: 69.4 us -> 68.2 us
    pallas_call x1, Pallas kernels: 69.4 us -> 68.2 us  [body(): pl.pallas_call(kernel, out_shape=jax.ShapeDtypeStruct((8, NCH, NS), F32),...]
where the time goes in v4:
time: 69.9 us; the launch traced here: 69.8 us
  Pallas kernels  68.2 us (98%)
  local copies, waits for them, and re-layouts  1.57 us (2%)
    pallas_call x1, Pallas kernels, body(): pl.pallas_call(kernel, out_shape=jax.ShapeDtypeStruct((8, NCH, NS), F32),...  68.2 us
    unnamed x1, local copies, waits for them, and re-layouts  1.57 us

profile of v4, /device:TPU:1, one launch (start us, length us, event | category | flops | bytes accessed | tf_op | source)
XLA Modules:
  0.0 69.8 jit_solution(11246486567252900272)
XLA Ops:
  0.0 68.2 %shard_map.46 = f32[8,8,512]{2,1,0:T(8,128)} custom-call(f32[8,8,2,4096]{3,2,1,0:T(2,128)} %vis_hbm.1, f32[8,8,2,4096]{3,2,1,0:T(2,128)} %model_hbm.1, s32[2,4096]{1,0:T(2,128)} %pairs.1, f32[8,8,512]{2,1,0:T(8,128)} %init.1), custom_call_target="tpu_custom_call" | custom-call | tf_op jit(solution)/shard_map/pallas_call | solution.py:394
  68.2 1.6 %copy.6 = f32[8,8,512]{2,1,0:T(8,128)} copy(f32[8,8,512]{2,1,0:T(8,128)} %shard_map.46) | data formatting | bytes 262144
